TPU v7x, 128 devices: a whole 4x4x4 slice. The times are simulated.
128 devices in a mesh: gx: 8 (over z_lo, x), gy: 16 (over z_hi, y, core).
Axes of the slice: x: 4, y: 4, z: 4 (z_hi: 2, z_lo: 2; z = z_hi * 2 + z_lo), core: 2. Of those that a mesh axis runs over, the one named last changes fastest.
Arguments:
- flow: float32 [27, 128, 256, 256], P(None, 'gx', 'gy'), may hold values from 0.05 to 0.45
- warmth_populace: float32 [7, 128, 256, 256], P(None, 'gx', 'gy'), as said below
- cell_type: int32 [128, 256, 256], P('gx', 'gy'), may hold values from 0 to 1
Outputs:
- flow_next: float32 [27, 128, 256, 256], P(None, 'gx', 'gy')
- heat_next: float32 [7, 128, 256, 256], P(None, 'gx', 'gy')
- heat_flux: float32 [], replicated
Inputs may be any that keep to these rules, and one draw needn't show every extreme that they name: `warmth_populace`: every population is positive.
All inputs are finite; a program needn't handle non-finite values.
Results may differ from a plain program's by a relative error of at most 0.0003.
Values sent between devices are 32-bit elements; how exact they have to be, the bound alone decides.
A program may use at most 128 MiB of HBM per device.

v0:
```python
import functools

import jax
import jax.numpy as jnp
from jax import lax
from jax.experimental import pallas as pl
from jax.experimental.pallas import tpu as pltpu
from jax.sharding import PartitionSpec as P

MESH = pl.DeviceIdType.MESH
STEPS = 2
LANES = 128
ROWS = 8

PAIRS = [
    (a, b, e)
    for a in (-1, 0, 1)
    for b in (-1, 0, 1)
    for e in (-1, 0, 1)
    if (a, b, e) > (0, 0, 0)
]
HEAT_MOVES = [(0, 0, 0), (1, 0, 0), (-1, 0, 0), (0, 1, 0), (0, -1, 0), (0, 0, 1), (0, 0, -1)]
TAU_COOLANT = 0.5 + 4.0 * 0.05
TAU_METAL = 0.5 + 4.0 * 0.25
FACES = [(1, 0), (-1, 0)]
SIDES = [(0, 1), (0, -1)]
CORNERS = [(1, 1), (1, -1), (-1, 1), (-1, -1)]


def first_plane(a):
    return 1 if a == 1 else 0


def first_row(b):
    return ROWS if b == 1 else 0


def tree(terms):
    terms = list(terms)
    while len(terms) > 1:
        terms = [
            terms[k] + terms[k + 1] if k + 1 < len(terms) else terms[k]
            for k in range(0, len(terms), 2)
        ]
    return terms[0]


def signed(terms):
    plus = tree([value for sign, value in terms if sign > 0])
    minus = [value for sign, value in terms if sign < 0]
    return plus - tree(minus) if minus else plus


def inverse(value):
    guess = pl.reciprocal(value, approx=True)
    return guess * (2.0 - value * guess)


def lane_shift(pair, e, lane):
    if e == 0:
        return pair
    turned = [pltpu.roll(half, 1 if e == 1 else LANES - 1, 1) for half in pair]
    at_end = lane == (0 if e == 1 else LANES - 1)
    return [jnp.where(at_end, turned[1 - k], turned[k]) for k in range(2)]


def collide(rest, sums, diffs, heat, fluid):
    density = tree([rest] + sums)
    moments = [
        signed([(c[axis], diffs[k]) for k, c in enumerate(PAIRS) if c[axis] != 0])
        for axis in range(3)
    ]
    warmth = tree(heat)
    rate = inverse(0.5 + 0.15 * jnp.exp(0.5 - 0.5 * warmth))
    rate = jnp.where(fluid, rate, 0.0)
    scale = jnp.where(fluid, inverse(density) * 3.0, 0.0)
    vx, vy, vz = [moment * scale for moment in moments]
    keep = 0.5 - 0.5 * rate
    turn = jnp.where(fluid, keep, -0.5)
    weight = rate * density
    sx, sy, sz = (0.5 * vx) * vx, (0.5 * vy) * vy, (0.5 * vz) * vz
    total = sx + sy + sz
    base = 1.0 - total * (1.0 / 3.0)
    k1 = weight * (2.0 / 27.0)
    k2 = weight * (1.0 / 54.0)
    k3 = weight * (1.0 / 216.0)
    halves = {}
    speed = (vx, vy, vz)
    square = (sx, sy, sz)
    for axis in range(3):
        c = tuple(1 if n == axis else 0 for n in range(3))
        halves[c] = (k1 * (base + square[axis]), k1 * speed[axis])
    k2v = [k2 * v for v in speed]
    for m, n in ((0, 1), (0, 2), (1, 2)):
        even = k2 * (base + square[m] + square[n])
        cross = k2v[m] * speed[n]
        for sign in (1, -1):
            c = [0, 0, 0]
            c[m], c[n] = 1, sign
            halves[tuple(c)] = (
                (even + cross, k2v[m] + k2v[n]) if sign == 1 else (even - cross, k2v[m] - k2v[n])
            )
    k3v = [k3 * v for v in speed]
    even = k3 * (base + total)
    xy, xz, yz = k3v[0] * vy, k3v[0] * vz, k3v[1] * vz
    for b in (1, -1):
        outer = even + xy if b == 1 else even - xy
        inner = xz + yz if b == 1 else xz - yz
        slope = k3v[0] + k3v[1] if b == 1 else k3v[0] - k3v[1]
        for e in (1, -1):
            halves[(1, b, e)] = (
                (outer + inner, slope + k3v[2]) if e == 1 else (outer - inner, slope - k3v[2])
            )
    out_rest = (keep + keep) * rest + (weight * (8.0 / 27.0)) * base
    out_pairs = []
    for k, c in enumerate(PAIRS):
        even, odd = halves[c]
        even = keep * sums[k] + even
        odd = turn * diffs[k] + odd
        out_pairs.append((even + odd, even - odd))
    heat_rate = jnp.where(fluid, 1.0 / TAU_COOLANT, 1.0 / TAU_METAL)
    heat_keep = 1.0 - heat_rate
    part = (heat_rate * 0.125) * warmth
    slant = part * (4.0 / 3.0)
    hot = [heat_keep * heat[0] + (part + part)]
    for axis in range(3):
        lean = slant * speed[axis]
        hot.append(heat_keep * heat[1 + 2 * axis] + (part + lean))
        hot.append(heat_keep * heat[2 + 2 * axis] + (part - lean))
    return out_rest, out_pairs, hot


def step_kernel(
    nx, ny, flow_hbm, heat_hbm, kind_hbm, flow_out, heat_out, flux_out,
    flow_in, heat_in, kind, lines, bits, weights, cold_a, cold_b, warm_a, warm_b, meet, meet2, flux_ref,
    in_sem, kind_sem, send_sem, recv_sem, ksend_sem, krecv_sem, sum_sem, sum_recv,
):
    gx, gy = lax.axis_index("gx"), lax.axis_index("gy")
    planes = flow_in.shape[1]
    height = flow_in.shape[2]
    lane = lax.broadcasted_iota(jnp.int32, (ROWS, LANES), 1)
    half = height // ROWS

    def plane_of(p):
        return lax.rem(p, 2) * (planes - 1 - p // 2) + (1 - lax.rem(p, 2)) * (p // 2)

    def device(dx, dy):
        return (lax.rem(gx + dx + nx, nx), lax.rem(gy + dy + ny, ny))

    def inside(dy, act):
        if dy == 1:
            pl.when(gy < ny - 1)(act)
        elif dy == -1:
            pl.when(gy > 0)(act)
        else:
            act()

    kind_copies = [
        pltpu.make_async_copy(
            kind_hbm.at[:, :, pl.ds(z * LANES, LANES)],
            kind.at[pl.ds(1, planes), z, pl.ds(ROWS, height), :],
            kind_sem.at[z],
        )
        for z in range(2)
    ]
    for copy in kind_copies:
        copy.start()

    def load(p):
        x = plane_of(p)
        return [
            pltpu.make_async_copy(
                flow_hbm.at[:, pl.ds(x, 1)], flow_in.at[:, pl.ds(x, 1)], in_sem.at[0, p]
            ),
            pltpu.make_async_copy(
                heat_hbm.at[:, pl.ds(x, 1)], heat_in.at[:, pl.ds(x, 1)], in_sem.at[1, p]
            ),
        ]

    def load_all(p, carry):
        for copy in load(p):
            copy.start()
        return carry

    lax.fori_loop(0, planes, load_all, 0)

    barrier = pltpu.get_barrier_semaphore()
    for dx, dy in CORNERS:
        pl.semaphore_signal(barrier, inc=1, device_id=device(dx, dy), device_id_type=MESH)
    for d in range(1, nx):
        pl.semaphore_signal(barrier, inc=1, device_id=device(d, 0), device_id_type=MESH)
    for d in range(1, ny):
        pl.semaphore_signal(barrier, inc=1, device_id=device(0, d), device_id_type=MESH)

    for copy in kind_copies:
        copy.wait()

    def kind_copy(n, dx, dy):
        src_x = {1: pl.ds(planes, 1), -1: pl.ds(1, 1), 0: pl.ds(1, planes)}[dx]
        dst_x = {1: pl.ds(0, 1), -1: pl.ds(planes + 1, 1), 0: pl.ds(1, planes)}[dx]
        src_y = {1: pl.ds(ROWS + height - 1, 1), -1: pl.ds(ROWS, 1), 0: pl.ds(ROWS, height)}[dy]
        dst_y = {1: pl.ds(ROWS - 1, 1), -1: pl.ds(ROWS + height, 1), 0: pl.ds(ROWS, height)}[dy]
        return pltpu.make_async_remote_copy(
            src_ref=kind.at[src_x, :, src_y, :],
            dst_ref=kind.at[dst_x, :, dst_y, :],
            send_sem=ksend_sem.at[n],
            recv_sem=krecv_sem.at[n],
            device_id=device(dx, dy),
            device_id_type=MESH,
        )

    kind_list = [(n, dx, dy) for n, (dx, dy) in enumerate(FACES + SIDES + CORNERS)]

    def face_copies(turn, cold, warm, dx):
        n = 0 if dx == 1 else 1
        a = dx + 1
        src = planes if dx == 1 else 0
        dst = 0 if dx == 1 else planes
        j = 1 if dx == 1 else 2
        return [
            pltpu.make_async_remote_copy(
                src_ref=cold.at[a, b, :, src, :, pl.ds(first_row(b - 1), height), :],
                dst_ref=cold.at[a, b, :, dst, :, pl.ds(first_row(b - 1), height), :],
                send_sem=send_sem.at[turn, 4 * n + b],
                recv_sem=recv_sem.at[turn, 4 * n + b],
                device_id=device(dx, 0),
                device_id_type=MESH,
            )
            for b in range(3)
        ] + [
            pltpu.make_async_remote_copy(
                src_ref=warm.at[j, src, :, pl.ds(0, height), :],
                dst_ref=warm.at[j, dst, :, pl.ds(0, height), :],
                send_sem=send_sem.at[turn, 4 * n + 3],
                recv_sem=recv_sem.at[turn, 4 * n + 3],
                device_id=device(dx, 0),
                device_id_type=MESH,
            )
        ]

    def corner_copy(turn, cold, dx, dy):
        n = 8 + CORNERS.index((dx, dy))
        src = planes if dx == 1 else 0
        dst = 0 if dx == 1 else planes
        src_y = ROWS + height - 1 if dy == 1 else 0
        dst_y = ROWS - 1 if dy == 1 else height
        return pltpu.make_async_remote_copy(
            src_ref=cold.at[dx + 1, dy + 1, :, src, :, pl.ds(src_y, 1), :],
            dst_ref=cold.at[dx + 1, dy + 1, :, dst, :, pl.ds(dst_y, 1), :],
            send_sem=send_sem.at[turn, n],
            recv_sem=recv_sem.at[turn, n],
            device_id=device(dx, dy),
            device_id_type=MESH,
        )

    group = 2

    def side_copies(turn, cold, warm, dy, g):
        src_y = ROWS + height - 1 if dy == 1 else 0
        dst_y = ROWS - 1 if dy == 1 else height
        j = 3 if dy == 1 else 4
        at = 12 + 4 * (planes // group) * (0 if dy == 1 else 1) + 4 * g
        copies = []
        for a in range(3):
            xs = pl.ds(first_plane(a - 1) + group * g, group)
            copies.append(
                pltpu.make_async_remote_copy(
                    src_ref=cold.at[a, dy + 1, :, xs, :, pl.ds(src_y, 1), :],
                    dst_ref=cold.at[a, dy + 1, :, xs, :, pl.ds(dst_y, 1), :],
                    send_sem=send_sem.at[turn, at + a],
                    recv_sem=recv_sem.at[turn, at + a],
                    device_id=device(0, dy),
                    device_id_type=MESH,
                )
            )
        xs = pl.ds(group * g, group)
        copies.append(
            pltpu.make_async_remote_copy(
                src_ref=warm.at[j, xs, :, pl.ds(src_y, 1), :],
                dst_ref=warm.at[j, xs, :, pl.ds(dst_y, 1), :],
                send_sem=send_sem.at[turn, at + 3],
                recv_sem=recv_sem.at[turn, at + 3],
                device_id=device(0, dy),
                device_id_type=MESH,
            )
        )
        return copies

    def start_all(copies):
        def act():
            for copy in copies:
                copy.start()
        return act

    def wait_recv_all(copies):
        def act():
            for copy in copies:
                copy.wait_recv()
        return act

    def wait_send_all(copies):
        def act():
            for copy in copies:
                copy.wait_send()
        return act

    def send_faces(turn, cold, warm):
        for dx, _ in FACES:
            start_all(face_copies(turn, cold, warm, dx))()
        for dx, dy in CORNERS:
            inside(dy, start_all([corner_copy(turn, cold, dx, dy)]))

    def take_faces(turn, cold, warm):
        for dx, _ in FACES:
            wait_recv_all(face_copies(turn, cold, warm, dx))()
        for dx, dy in CORNERS:
            inside(-dy, wait_recv_all([corner_copy(turn, cold, dx, dy)]))

    def send_sides(turn, cold, warm, g):
        for _, dy in SIDES:
            inside(dy, start_all(side_copies(turn, cold, warm, dy, g)))

    def take_sides(turn, cold, warm, g):
        for _, dy in SIDES:
            inside(-dy, wait_recv_all(side_copies(turn, cold, warm, dy, g)))

    groups = planes // group

    def sends_after(p, turn, cold, warm):
        @pl.when(p == 1)
        def _():
            send_faces(turn, cold, warm)

        @pl.when(lax.rem(p, 2 * group) == 2 * group - 1)
        def _():
            g = p // (2 * group)
            send_sides(turn, cold, warm, g)
            send_sides(turn, cold, warm, groups - 1 - g)

    def takes_before(p, turn, cold, warm):
        @pl.when(p == 0)
        def _():
            take_faces(turn, cold, warm)
            take_sides(turn, cold, warm, 0)
            take_sides(turn, cold, warm, groups - 1)

        @pl.when((lax.rem(p, 2 * group) == 2 * group - 2) & (p < planes - group))
        def _():
            g = p // (2 * group) + 1
            take_sides(turn, cold, warm, g)
            take_sides(turn, cold, warm, groups - 1 - g)

    def store(cold, warm, x, r, z, rest, pairs, hot):
        cold[1, 1, 1, x, z, pl.ds(r, ROWS), :] = rest
        for (a, b, e), (ahead, back) in zip(PAIRS, pairs):
            for (ca, cb, ce), value in (((a, b, e), ahead), ((-a, -b, -e), back)):
                cold[ca + 1, cb + 1, ce + 1, x + first_plane(ca), z, pl.ds(r + first_row(cb), ROWS), :] = value
        for j, (a, b, e) in enumerate(HEAT_MOVES):
            warm[j, x + first_plane(a), z, pl.ds(r + first_row(b), ROWS), :] = hot[j]

    def wall_rows(warm, x):
        @pl.when(gy == 0)
        def _():
            for z in range(2):
                warm[3, x, z, pl.ds(ROWS - 1, 1), :] = warm[4, x, z, pl.ds(0, 1), :]

        @pl.when(gy == ny - 1)
        def _():
            for z in range(2):
                warm[4, x, z, pl.ds(height, 1), :] = warm[3, x, z, pl.ds(ROWS + height - 1, 1), :]

    def first(p, carry):
        x = plane_of(p)
        for copy in load(p):
            copy.wait()

        @pl.when(p == 1)
        def _():
            pl.semaphore_wait(barrier, len(CORNERS) + nx - 1 + ny - 1)
            for n, dx, dy in kind_list:
                inside(dy, kind_copy(n, dx, dy).start)

        def unit(h, carry):
            r = pl.multiple_of(h * ROWS, ROWS)
            for z in range(2):
                at = (x, pl.ds(r, ROWS), pl.ds(z * LANES, LANES))
                values = [flow_in[(i,) + at] for i in range(27)]
                heat = [heat_in[(j,) + at] for j in range(7)]
                fluid = kind[x + 1, z, pl.ds(r + ROWS, ROWS), :] == 0
                sums = [values[i] + values[26 - i] for i in range(14, 27)]
                diffs = [values[i] - values[26 - i] for i in range(14, 27)]
                rest, pairs, hot = collide(values[13], sums, diffs, heat, fluid)
                store(cold_a, warm_a, x, r, z, rest, pairs, hot)
            return carry

        lax.fori_loop(0, half, unit, 0)
        wall_rows(warm_a, x)
        sends_after(p, 0, cold_a, warm_a)
        return carry

    lax.fori_loop(0, planes, first, 0)

    for n, dx, dy in kind_list:
        inside(-dy, kind_copy(n, dx, dy).wait_recv)

    def outside_rows(row):
        def act():
            kind[:, :, pl.ds(row, 1), :] = jnp.full((planes + 2, 2, 1, LANES), 2, jnp.int32)
        return act

    pl.when(gy == 0)(outside_rows(ROWS - 1))
    pl.when(gy == ny - 1)(outside_rows(ROWS + height))

    def line(u, carry):
        x, r = u // (half + 2), pl.multiple_of(lax.rem(u, half + 2) * ROWS, ROWS)
        here = [(kind[x, z, pl.ds(r, ROWS), :] == 0).astype(jnp.int32) for z in range(2)]
        above = lane_shift(here, -1, lane)
        below = lane_shift(here, 1, lane)
        for z in range(2):
            lines[x, z, pl.ds(r, ROWS), :] = above[z] + 2 * here[z] + 4 * below[z]
        return carry

    lax.fori_loop(0, (planes + 2) * (half + 2), line, 0)

    def mask(u, carry):
        x, r = u // half, pl.multiple_of(lax.rem(u, half) * ROWS, ROWS)
        own = [kind[x + 1, z, pl.ds(r + ROWS, ROWS), :] for z in range(2)]
        around = [
            [kind[x + 2, z, pl.ds(r + ROWS, ROWS), :] for z in range(2)],
            [kind[x, z, pl.ds(r + ROWS, ROWS), :] for z in range(2)],
            [kind[x + 1, z, pl.ds(r + ROWS + 1, ROWS), :] for z in range(2)],
            [kind[x + 1, z, pl.ds(r + ROWS - 1, ROWS), :] for z in range(2)],
            lane_shift(own, -1, lane),
            lane_shift(own, 1, lane),
        ]
        for z in range(2):
            found = jnp.zeros((ROWS, LANES), jnp.int32)
            for a in (-1, 0, 1):
                for b in (-1, 0, 1):
                    found = found + (
                        lines[x + 1 - a, z, pl.ds(r + ROWS - b, ROWS), :] << (9 * (a + 1) + 3 * (b + 1))
                    )
            bits[x, z, pl.ds(r, ROWS), :] = jnp.where(own[z] == 0, found, 0)
            for j in range(6):
                other = jnp.where(around[j][z] == 2, own[z], around[j][z])
                weights[j, x, z, pl.ds(r, ROWS), :] = (own[z] - other).astype(jnp.float32)
        return carry

    lax.fori_loop(0, planes * half, mask, 0)

    def arrive(cold, x, r, code, c):
        a, b, e = c
        number = 9 * (a + 1) + 3 * (b + 1) + (e + 1)
        found = [
            cold[a + 1, b + 1, e + 1, x + first_plane(a) - a, z, pl.ds(r + first_row(b) - b, ROWS), :]
            for z in range(2)
        ]
        found = lane_shift(found, e, lane)
        return [
            jnp.where(
                (code[z] & (1 << number)) != 0,
                found[z],
                cold[1 - a, 1 - b, 1 - e, x + first_plane(-a), z, pl.ds(r + first_row(-b), ROWS), :],
            )
            for z in range(2)
        ]

    def arrive_heat(warm, x, r, j):
        a, b, e = HEAT_MOVES[j]
        found = [
            warm[j, x + first_plane(a) - a, z, pl.ds(r + first_row(b) - b, ROWS), :] for z in range(2)
        ]
        return lane_shift(found, e, lane)

    flux_ref[...] = jnp.zeros_like(flux_ref)

    def second(p, carry):
        x = plane_of(p)
        takes_before(p, 0, cold_a, warm_a)

        def unit(h, carry):
            r = pl.multiple_of(h * ROWS, ROWS)
            code = [bits[x, z, pl.ds(r, ROWS), :] for z in range(2)]
            rest = [cold_a[1, 1, 1, x, z, pl.ds(r, ROWS), :] for z in range(2)]
            sums, diffs = [], []
            for a, b, e in PAIRS:
                ahead = arrive(cold_a, x, r, code, (a, b, e))
                back = arrive(cold_a, x, r, code, (-a, -b, -e))
                sums.append([ahead[z] + back[z] for z in range(2)])
                diffs.append([ahead[z] - back[z] for z in range(2)])
            heat = [arrive_heat(warm_a, x, r, j) for j in range(7)]
            flux = flux_ref[...]
            for z in range(2):
                fluid = kind[x + 1, z, pl.ds(r + ROWS, ROWS), :] == 0
                out_rest, pairs, hot = collide(
                    rest[z], [s[z] for s in sums], [d[z] for d in diffs], [g[z] for g in heat], fluid
                )
                store(cold_b, warm_b, x, r, z, out_rest, pairs, hot)
                terms = []
                for j in range(1, 7):
                    a, b, e = HEAT_MOVES[j]
                    was = warm_a[j, x + first_plane(a), z, pl.ds(r + first_row(b), ROWS), :]
                    terms.append(weights[j - 1, x, z, pl.ds(r, ROWS), :] * (was + hot[j]))
                flux = flux + tree(terms)
            flux_ref[...] = flux
            return carry

        lax.fori_loop(0, half, unit, 0)
        wall_rows(warm_b, x)
        sends_after(p, 1, cold_b, warm_b)
        return carry

    lax.fori_loop(0, planes, second, 0)

    def sum_copies(slots, stage, axis, index, count):
        return [
            pltpu.make_async_remote_copy(
                src_ref=slots.at[index],
                dst_ref=slots.at[index],
                send_sem=sum_sem.at[stage, d - 1],
                recv_sem=sum_recv.at[stage, d - 1],
                device_id=device(d, 0) if axis == 0 else device(0, d),
                device_id_type=MESH,
            )
            for d in range(1, count)
        ]

    meet[gy] = flux_ref[...]
    column = sum_copies(meet, 0, 1, gy, ny)
    start_all(column)()

    def third(p, carry):
        x = plane_of(p)
        takes_before(p, 1, cold_b, warm_b)

        def unit(h, carry):
            r = pl.multiple_of(h * ROWS, ROWS)
            code = [bits[x, z, pl.ds(r, ROWS), :] for z in range(2)]
            for a in (-1, 0, 1):
                for b in (-1, 0, 1):
                    for e in (-1, 0, 1):
                        i = 9 * (a + 1) + 3 * (b + 1) + (e + 1)
                        if i == 13:
                            value = [cold_b[1, 1, 1, x, z, pl.ds(r, ROWS), :] for z in range(2)]
                        else:
                            value = arrive(cold_b, x, r, code, (a, b, e))
                        for z in range(2):
                            flow_out[i, x, pl.ds(r, ROWS), pl.ds(z * LANES, LANES)] = value[z]
            for j in range(7):
                value = arrive_heat(warm_b, x, r, j)
                for z in range(2):
                    heat_out[j, x, pl.ds(r, ROWS), pl.ds(z * LANES, LANES)] = value[z]
            return carry

        lax.fori_loop(0, half, unit, 0)

        @pl.when(p == planes // 2)
        def _():
            for copy in column:
                copy.wait_recv()
            meet2[gx] = tree([meet[n] for n in range(ny)])
            for copy in sum_copies(meet2, 1, 0, gx, nx):
                copy.start()

        return carry

    lax.fori_loop(0, planes, third, 0)

    row = sum_copies(meet2, 1, 0, gx, nx)
    for copy in row:
        copy.wait_recv()
    flux_out[...] = tree([meet2[n] for n in range(nx)])

    for copy in column + row:
        copy.wait_send()
    for n, dx, dy in kind_list:
        inside(dy, kind_copy(n, dx, dy).wait_send)
    for turn, cold, warm in ((0, cold_a, warm_a), (1, cold_b, warm_b)):
        for dx, _ in FACES:
            wait_send_all(face_copies(turn, cold, warm, dx))()
        for dx, dy in CORNERS:
            inside(dy, wait_send_all([corner_copy(turn, cold, dx, dy)]))

        def drain(g, carry, turn=turn, cold=cold, warm=warm):
            for _, dy in SIDES:
                inside(dy, wait_send_all(side_copies(turn, cold, warm, dy, g)))
            return carry

        lax.fori_loop(0, groups, drain, 0)


def out_kernel(cells, flow_ref, heat_ref, flux_ref, flow_out, heat_out, total_out, sem):
    copies = [
        pltpu.make_async_copy(flow_ref, flow_out, sem.at[0]),
        pltpu.make_async_copy(heat_ref, heat_out, sem.at[1]),
    ]
    for copy in copies:
        copy.start()
    total_out[0, 0] = jnp.sum(flux_ref[...]) * (1.0 / cells)
    for copy in copies:
        copy.wait()


def per_device(nx, ny, flow, heat, kind):
    _, planes, height, length = flow.shape
    assert length == 2 * LANES and height % ROWS == 0 and planes % 4 == 0
    cold = (3, 3, 3, planes + 1, 2, height + ROWS, LANES)
    warm = (7, planes + 1, 2, height + ROWS, LANES)
    padded = (planes + 2, 2, height + 2 * ROWS, LANES)
    f32, i32 = jnp.float32, jnp.int32
    copies = 12 + 2 * 4 * (planes // 2)
    flow_new, heat_new, flux = pl.pallas_call(
        functools.partial(step_kernel, nx, ny),
        out_shape=(
            pltpu.VMEM(flow.shape, f32),
            pltpu.VMEM(heat.shape, f32),
            pltpu.VMEM((ROWS, LANES), f32),
        ),
        in_specs=[pl.BlockSpec(memory_space=pl.ANY)] * 3,
        out_specs=[pl.BlockSpec(memory_space=pltpu.VMEM)] * 3,
        scratch_shapes=[
            pltpu.VMEM(flow.shape, f32),
            pltpu.VMEM(heat.shape, f32),
            pltpu.VMEM(padded, i32),
            pltpu.VMEM(padded, i32),
            pltpu.VMEM((planes, 2, height, LANES), i32),
            pltpu.VMEM((6, planes, 2, height, LANES), f32),
            pltpu.VMEM(cold, f32),
            pltpu.VMEM(cold, f32),
            pltpu.VMEM(warm, f32),
            pltpu.VMEM(warm, f32),
            pltpu.VMEM((ny, ROWS, LANES), f32),
            pltpu.VMEM((nx, ROWS, LANES), f32),
            pltpu.VMEM((ROWS, LANES), f32),
            pltpu.SemaphoreType.DMA((2, planes)),
            pltpu.SemaphoreType.DMA((2,)),
            pltpu.SemaphoreType.DMA((2, copies)),
            pltpu.SemaphoreType.DMA((2, copies)),
            pltpu.SemaphoreType.DMA((8,)),
            pltpu.SemaphoreType.DMA((8,)),
            pltpu.SemaphoreType.DMA((2, max(nx, ny))),
            pltpu.SemaphoreType.DMA((2, max(nx, ny))),
        ],
        compiler_params=pltpu.CompilerParams(
            collective_id=0, has_side_effects=True, vmem_limit_bytes=50 * 1024 * 1024
        ),
    )(flow, heat, kind)
    cells = float(planes * nx * height * ny)
    flow_new, heat_new, total = pl.pallas_call(
        functools.partial(out_kernel, cells),
        out_shape=(
            jax.ShapeDtypeStruct(flow.shape, f32),
            jax.ShapeDtypeStruct(heat.shape, f32),
            jax.ShapeDtypeStruct((1, 1), f32),
        ),
        in_specs=[pl.BlockSpec(memory_space=pltpu.VMEM)] * 3,
        out_specs=[
            pl.BlockSpec(memory_space=pl.ANY),
            pl.BlockSpec(memory_space=pl.ANY),
            pl.BlockSpec(memory_space=pltpu.SMEM),
        ],
        scratch_shapes=[pltpu.SemaphoreType.DMA((2,))],
        compiler_params=pltpu.CompilerParams(vmem_limit_bytes=1024 * 1024),
    )(*[pltpu.with_memory_space_constraint(v, pltpu.VMEM) for v in (flow_new, heat_new, flux)])
    return flow_new, heat_new, total[0, 0]


def solution(mesh):
    return jax.shard_map(
        functools.partial(per_device, mesh.shape["gx"], mesh.shape["gy"]),
        mesh=mesh,
        in_specs=(P(None, "gx", "gy", None), P(None, "gx", "gy", None), P("gx", "gy", None)),
        out_specs=(P(None, "gx", "gy", None), P(None, "gx", "gy", None), P()),
        check_vma=False,
    )
```

profile of v0, /device:TPU:1, one launch (start us, length us, event | category | flops | bytes accessed | tf_op | source)
XLA Modules:
  0.0 45.2 jit_solution(8829932701085663047)
XLA Ops:
  0.6 40.5 %shard_map.58 = (f32[27,16,16,256]{3,2,1,0:T(8,128)S(1)}, f32[7,16,16,256]{3,2,1,0:T(8,128)S(1)}, f32[8,128]{1,0:T(8,128)S(1)}) custom-call(f32[27,16,16,256]{3,2,1,0:T(8,128)} %flow_hbm.1, f32[7,16,16,256]{3,2,1,0:T(8,128)} %heat_hbm.1, s32[16,16,256]{2,1,0:T(8,128)} %kind_hbm.1), custom_call_target="tpu_custom_call" | custom-call | tf_op jit(solution)/shard_map/pallas_call | solution.py:612
  41.1 4.1 %shard_map.59 = (f32[27,16,16,256]{3,2,1,0:T(8,128)}, f32[7,16,16,256]{3,2,1,0:T(8,128)}, f32[1,1]{1,0:T(1,128)}) custom-call(f32[27,16,16,256]{3,2,1,0:T(8,128)S(1)} %get-tuple-element.9.flow_ref, f32[7,16,16,256]{3,2,1,0:T(8,128)S(1)} %get-tuple-element.10.heat_ref, f32[8,128]{1,0:T(8,128)S(1)} %get-tuple-element.11.flux_ref), custom_call_target="tpu_custom_call" | custom-call | tf_op jit(solution)/shard_map/pallas_call | solution.py:649
where the time goes:
time: 45.3 us; the launch traced here: 45.2 us
  Pallas kernels  44.6 us (98%)
  between operations  0.64 us (1%)
    pallas_call x1, Pallas kernels, per_device(): pl.pallas_call(functools.partial(step_kernel, nx, ny), out_shape=(pltpu.V...  40.5 us
    pallas_call x1, Pallas kernels, per_device(): pl.pallas_call(functools.partial(out_kernel, cells), out_shape=(jax.Shape...  4.09 us

commit v1 on v0

v1 whole, which is shorter than its diff:
```python
import functools

import jax
import jax.numpy as jnp
from jax import lax
from jax.experimental import pallas as pl
from jax.experimental.pallas import tpu as pltpu
from jax.sharding import PartitionSpec as P

MESH = pl.DeviceIdType.MESH
NEAR = 4
STEPS = 2
LANES = 128
ROWS = 8

PAIRS = [
    (a, b, e)
    for a in (-1, 0, 1)
    for b in (-1, 0, 1)
    for e in (-1, 0, 1)
    if (a, b, e) > (0, 0, 0)
]
HEAT_MOVES = [(0, 0, 0), (1, 0, 0), (-1, 0, 0), (0, 1, 0), (0, -1, 0), (0, 0, 1), (0, 0, -1)]
TAU_COOLANT = 0.5 + 4.0 * 0.05
TAU_METAL = 0.5 + 4.0 * 0.25
FACES = [(1, 0), (-1, 0)]
SIDES = [(0, 1), (0, -1)]
CORNERS = [(1, 1), (1, -1), (-1, 1), (-1, -1)]


def tree(terms):
    terms = list(terms)
    while len(terms) > 1:
        terms = [
            terms[k] + terms[k + 1] if k + 1 < len(terms) else terms[k]
            for k in range(0, len(terms), 2)
        ]
    return terms[0]


def signed(terms):
    plus = tree([value for sign, value in terms if sign > 0])
    minus = [value for sign, value in terms if sign < 0]
    return plus - tree(minus) if minus else plus


def inverse(value):
    guess = pl.reciprocal(value, approx=True)
    return guess * (2.0 - value * guess)


def lane_shift(pair, e, lane):
    if e == 0:
        return pair
    turned = [pltpu.roll(half, 1 if e == 1 else LANES - 1, 1) for half in pair]
    at_end = lane == (0 if e == 1 else LANES - 1)
    return [jnp.where(at_end, turned[1 - k], turned[k]) for k in range(2)]


def collide(rest, sums, diffs, heat, fluid):
    density = tree([rest] + sums)
    moments = [
        signed([(c[axis], diffs[k]) for k, c in enumerate(PAIRS) if c[axis] != 0])
        for axis in range(3)
    ]
    warmth = tree(heat)
    rate = inverse(0.5 + 0.15 * jnp.exp(0.5 - 0.5 * warmth))
    rate = jnp.where(fluid, rate, 0.0)
    scale = jnp.where(fluid, inverse(density) * 3.0, 0.0)
    vx, vy, vz = [moment * scale for moment in moments]
    keep = 0.5 - 0.5 * rate
    turn = jnp.where(fluid, keep, -0.5)
    weight = rate * density
    sx, sy, sz = (0.5 * vx) * vx, (0.5 * vy) * vy, (0.5 * vz) * vz
    total = sx + sy + sz
    base = 1.0 - total * (1.0 / 3.0)
    k1 = weight * (2.0 / 27.0)
    k2 = weight * (1.0 / 54.0)
    k3 = weight * (1.0 / 216.0)
    halves = {}
    speed = (vx, vy, vz)
    square = (sx, sy, sz)
    for axis in range(3):
        c = tuple(1 if n == axis else 0 for n in range(3))
        halves[c] = (k1 * (base + square[axis]), k1 * speed[axis])
    k2v = [k2 * v for v in speed]
    for m, n in ((0, 1), (0, 2), (1, 2)):
        even = k2 * (base + square[m] + square[n])
        cross = k2v[m] * speed[n]
        for sign in (1, -1):
            c = [0, 0, 0]
            c[m], c[n] = 1, sign
            halves[tuple(c)] = (
                (even + cross, k2v[m] + k2v[n]) if sign == 1 else (even - cross, k2v[m] - k2v[n])
            )
    k3v = [k3 * v for v in speed]
    even = k3 * (base + total)
    xy, xz, yz = k3v[0] * vy, k3v[0] * vz, k3v[1] * vz
    for b in (1, -1):
        outer = even + xy if b == 1 else even - xy
        inner = xz + yz if b == 1 else xz - yz
        slope = k3v[0] + k3v[1] if b == 1 else k3v[0] - k3v[1]
        for e in (1, -1):
            halves[(1, b, e)] = (
                (outer + inner, slope + k3v[2]) if e == 1 else (outer - inner, slope - k3v[2])
            )
    out_rest = (keep + keep) * rest + (weight * (8.0 / 27.0)) * base
    out_pairs = []
    for k, c in enumerate(PAIRS):
        even, odd = halves[c]
        even = keep * sums[k] + even
        odd = turn * diffs[k] + odd
        out_pairs.append((even + odd, even - odd))
    heat_rate = jnp.where(fluid, 1.0 / TAU_COOLANT, 1.0 / TAU_METAL)
    heat_keep = 1.0 - heat_rate
    part = (heat_rate * 0.125) * warmth
    slant = part * (4.0 / 3.0)
    hot = [heat_keep * heat[0] + (part + part)]
    for axis in range(3):
        lean = slant * speed[axis]
        hot.append(heat_keep * heat[1 + 2 * axis] + (part + lean))
        hot.append(heat_keep * heat[2 + 2 * axis] + (part - lean))
    return out_rest, out_pairs, hot


def step_kernel(
    nx, ny, flow_hbm, heat_hbm, kind_hbm, flow_buf, heat_buf, flux_out,
    kind, bits, weights, cold_a, cold_b, warm_a, warm_b, meet_column, meet_layer, flux_ref,
    in_sem, kind_sem, send_sem, recv_sem, kind_send, kind_recv, sum_send, sum_recv,
):
    gx, gy = lax.axis_index("gx"), lax.axis_index("gy")
    planes, height = flow_buf.shape[1], flow_buf.shape[2]
    lane = lax.broadcasted_iota(jnp.int32, (ROWS, LANES), 1)
    half = height // ROWS
    low_row, high_row = ROWS, ROWS + height - 1

    def outer_first(p):
        k = p // 2
        return lax.rem(p, 2) * (planes - 1 - k) + (1 - lax.rem(p, 2)) * k

    def outer_third(p):
        k = p // 2
        k = jnp.where(k < 3, lax.rem(k + 1, 3), k)
        return lax.rem(p, 2) * (planes - 1 - k) + (1 - lax.rem(p, 2)) * k

    def row_groups(p):
        low = lax.shift_right_logical(p, 6) * ROWS
        return [pl.multiple_of(low + h * ROWS, ROWS) for h in range(half)]

    def device(dx, dy):
        return (lax.rem(gx + dx + nx, nx), lax.rem(gy + dy + ny, ny))

    def inside(dy, act):
        if dy == 1:
            pl.when(gy < ny - 1)(act)
        elif dy == -1:
            pl.when(gy > 0)(act)
        else:
            act()

    kind_copies = [
        pltpu.make_async_copy(
            kind_hbm.at[:, :, pl.ds(z * LANES, LANES)],
            kind.at[pl.ds(1, planes), z, pl.ds(low_row, height), :],
            kind_sem.at[z],
        )
        for z in range(2)
    ]
    for copy in kind_copies:
        copy.start()

    def load(k):
        xs = pl.ds(2 * k, 2)
        return [
            pltpu.make_async_copy(flow_hbm.at[:, xs], flow_buf.at[:, xs], in_sem.at[0, k]),
            pltpu.make_async_copy(heat_hbm.at[:, xs], heat_buf.at[:, xs], in_sem.at[1, k]),
        ]

    for k in range(planes // 4):
        for copy in load(k) + load(planes // 2 - 1 - k):
            copy.start()

    along, across = gx // NEAR, lax.rem(gx, NEAR)
    far, near, core = gy // (2 * NEAR), lax.rem(gy, 2 * NEAR) // 2, lax.rem(gy, 2)
    fars = ny // (2 * NEAR)
    columns = 2 * fars * (nx // NEAR)
    layers = NEAR * NEAR
    column_index = (along * fars + far) * 2 + core
    layer_index = across * NEAR + near

    def column_device(d):
        n = lax.rem(column_index + d, columns)
        return ((n // (2 * fars)) * NEAR + across, (lax.rem(n, 2 * fars) // 2) * 2 * NEAR + near * 2 + lax.rem(n, 2))

    def layer_device(d):
        n = lax.rem(layer_index + d, layers)
        return (along * NEAR + n // NEAR, far * 2 * NEAR + lax.rem(n, NEAR) * 2 + core)

    barrier = pltpu.get_barrier_semaphore()
    greeted = [device(dx, dy) for dx, dy in FACES + SIDES + CORNERS]
    greeted += [column_device(d) for d in range(1, columns)]
    greeted += [layer_device(d) for d in range(1, layers)]
    for target in greeted:
        pl.semaphore_signal(barrier, inc=1, device_id=target, device_id_type=MESH)

    for copy in kind_copies:
        copy.wait()

    def spans(dx, dy, xs):
        src_x = {1: pl.ds(planes, 1), -1: pl.ds(1, 1), 0: xs}[dx]
        dst_x = {1: pl.ds(0, 1), -1: pl.ds(planes + 1, 1), 0: xs}[dx]
        src_y = {1: pl.ds(high_row, 1), -1: pl.ds(low_row, 1), 0: pl.ds(low_row, height)}[dy]
        dst_y = {1: pl.ds(low_row - 1, 1), -1: pl.ds(high_row + 1, 1), 0: pl.ds(low_row, height)}[dy]
        return (src_x, src_y), (dst_x, dst_y)

    def remote(src, dst, send, recv, dx, dy):
        return pltpu.make_async_remote_copy(
            src_ref=src, dst_ref=dst, send_sem=send, recv_sem=recv,
            device_id=device(dx, dy), device_id_type=MESH,
        )

    every = pl.ds(1, planes)

    def kind_copy(n, dx, dy):
        (sx, sy), (tx, ty) = spans(dx, dy, every)
        return remote(
            kind.at[sx, :, sy, :], kind.at[tx, :, ty, :], kind_send.at[n], kind_recv.at[n], dx, dy
        )

    kind_list = [(n, dx, dy) for n, (dx, dy) in enumerate(FACES + SIDES + CORNERS)]

    def moving(cold, dx, dy, xs, ys):
        a = dx + 1 if dx else slice(None)
        b = dy + 1 if dy else slice(None)
        return cold.at[a, b, :, xs, :, ys, :]

    def flow_copy(turn, cold, dx, dy, send, recv, xs=every):
        (sx, sy), (tx, ty) = spans(dx, dy, xs)
        return remote(
            moving(cold, dx, dy, sx, sy), moving(cold, dx, dy, tx, ty),
            send_sem.at[turn, send], recv_sem.at[turn, recv], dx, dy,
        )

    def heat_copy(turn, warm, dx, dy, send, recv, xs=every):
        j = HEAT_MOVES.index((dx, dy, 0))
        (sx, sy), (tx, ty) = spans(dx, dy, xs)
        return remote(
            warm.at[j, sx, :, sy, :], warm.at[j, tx, :, ty, :],
            send_sem.at[turn, send], recv_sem.at[turn, recv], dx, dy,
        )

    def face_copies(turn, cold, warm, n):
        dx, _ = FACES[n]
        return [
            flow_copy(turn, cold, dx, 0, 2 * n, 2 * n),
            heat_copy(turn, warm, dx, 0, 2 * n + 1, 2 * n + 1),
        ]

    def corner_copy(turn, cold, n):
        dx, dy = CORNERS[n]
        return flow_copy(turn, cold, dx, dy, 4 + n, 4 + n)

    group = planes // 4

    def side_copies(turn, cold, warm, n, g=None):
        _, dy = SIDES[n]
        xs = every if g is None else pl.ds(1 + group * g, group)
        recv = 8 + 2 * (4 * n + (0 if g is None else g))
        return [
            flow_copy(turn, cold, 0, dy, 8 + 2 * n, recv, xs),
            heat_copy(turn, warm, 0, dy, 9 + 2 * n, recv + 1, xs),
        ]

    def each(copies, what):
        def act():
            for copy in copies:
                getattr(copy, what)()
        return act

    def faces(turn, cold, warm, what):
        sign = -1 if what == "wait_recv" else 1
        for n in range(2):
            each(face_copies(turn, cold, warm, n), what)()
        for n in range(4):
            inside(sign * CORNERS[n][1], each([corner_copy(turn, cold, n)], what))

    def sides(turn, cold, warm, gs, what):
        sign = -1 if what == "wait_recv" else 1
        for n in range(2):
            copies = [c for g in gs for c in side_copies(turn, cold, warm, n, g)]
            inside(sign * SIDES[n][1], each(copies, what))

    def store(cold, warm, x, r, z, rest, pairs, hot):
        def at(value, target, c):
            target[c + (x + 1, z, pl.ds(r + ROWS, ROWS), slice(None))] = value
        at(rest, cold, (1, 1, 1))
        for (a, b, e), (ahead, back) in zip(PAIRS, pairs):
            at(ahead, cold, (1 + a, 1 + b, 1 + e))
            at(back, cold, (1 - a, 1 - b, 1 - e))
        for j in range(7):
            at(hot[j], warm, (j,))

    def wall_rows(warm, x):
        @pl.when(gy == 0)
        def _():
            for z in range(2):
                warm[3, x + 1, z, pl.ds(low_row - 1, 1), :] = warm[4, x + 1, z, pl.ds(low_row, 1), :]

        @pl.when(gy == ny - 1)
        def _():
            for z in range(2):
                warm[4, x + 1, z, pl.ds(high_row + 1, 1), :] = warm[3, x + 1, z, pl.ds(high_row, 1), :]

    def outside_rows(row):
        def act():
            kind[:, :, pl.ds(row, 1), :] = jnp.full((planes + 2, 2, 1, LANES), 2, jnp.int32)
        return act

    together = 2

    def mask(q, carry):
        for x in [q * together + n for n in range(together)]:
            for r in row_groups(q):
                own = [kind[x + 1, z, pl.ds(r + ROWS, ROWS), :] for z in range(2)]
                lines, near = [], []
                for z in range(2):
                    found = {}
                    for a in (-1, 0, 1):
                        for b in (-1, 0, 1):
                            value = own[z] if a == b == 0 else kind[x + 1 - a, z, pl.ds(r + ROWS - b, ROWS), :]
                            found[a, b] = value
                    near.append([found[-1, 0], found[1, 0], found[0, -1], found[0, 1]])
                    lines.append(tree([
                        jnp.where(found[a, b] == 0, 1 << (9 * (a + 1) + 3 * (b + 1)), 0)
                        for a in (-1, 0, 1) for b in (-1, 0, 1)
                    ]))
                above = lane_shift(lines, -1, lane)
                below = lane_shift(lines, 1, lane)
                for z in range(2):
                    code = above[z] + (lines[z] << 1) + (below[z] << 2)
                    bits[x, z, pl.ds(r, ROWS), :] = jnp.where(own[z] == 0, code, 0)
                    others = [jnp.where(v == 2, own[z], v) for v in near[z]]
                    others += [1 - ((v[z] >> 12) & 1) for v in (above, below)]
                    for j in range(6):
                        weights[j, x, z, pl.ds(r, ROWS), :] = (own[z] - others[j]).astype(jnp.float32)
        return carry

    def first(p, carry):
        x = outer_first(p)

        @pl.when(lax.rem(p, 4) < 2)
        def _():
            for copy in load(x // 2):
                copy.wait()

        @pl.when(p == 1)
        def _():
            pl.semaphore_wait(barrier, len(greeted))
            for n, dx, dy in kind_list:
                inside(dy, kind_copy(n, dx, dy).start)

        for r in row_groups(p):
            for z in range(2):
                at = (x, pl.ds(r, ROWS), pl.ds(z * LANES, LANES))
                values = [flow_buf[(i,) + at] for i in range(27)]
                heat = [heat_buf[(j,) + at] for j in range(7)]
                fluid = kind[x + 1, z, pl.ds(r + ROWS, ROWS), :] == 0
                sums = [values[i] + values[26 - i] for i in range(14, 27)]
                diffs = [values[i] - values[26 - i] for i in range(14, 27)]
                rest, pairs, hot = collide(values[13], sums, diffs, heat, fluid)
                store(cold_a, warm_a, x, r, z, rest, pairs, hot)
        wall_rows(warm_a, x)

        @pl.when(p == 1)
        def _():
            faces(0, cold_a, warm_a, "start")

        @pl.when(p == planes // 2 - 1)
        def _():
            sides(0, cold_a, warm_a, (0, 3), "start")

        return carry

    lax.fori_loop(0, planes, first, 0)
    sides(0, cold_a, warm_a, (1, 2), "start")

    for n, dx, dy in kind_list:
        inside(-dy, kind_copy(n, dx, dy).wait_recv)
    pl.when(gy == 0)(outside_rows(low_row - 1))
    pl.when(gy == ny - 1)(outside_rows(high_row + 1))
    lax.fori_loop(0, planes // together, mask, 0)

    def arrive(cold, x, r, code, c):
        a, b, e = c
        number = 9 * (a + 1) + 3 * (b + 1) + (e + 1)
        found = lane_shift(
            [cold[a + 1, b + 1, e + 1, x + 1 - a, z, pl.ds(r + ROWS - b, ROWS), :] for z in range(2)],
            e, lane,
        )
        return [
            jnp.where(
                (code[z] & (1 << number)) != 0,
                found[z],
                cold[1 - a, 1 - b, 1 - e, x + 1, z, pl.ds(r + ROWS, ROWS), :],
            )
            for z in range(2)
        ]

    def arrive_heat(warm, x, r, j):
        a, b, e = HEAT_MOVES[j]
        found = [warm[j, x + 1 - a, z, pl.ds(r + ROWS - b, ROWS), :] for z in range(2)]
        return lane_shift(found, e, lane)

    def takes_before(p, turn, cold, warm):
        @pl.when(p == 0)
        def _():
            sides(turn, cold, warm, (0, 3), "wait_recv")

        @pl.when(p == 4)
        def _():
            faces(turn, cold, warm, "wait_recv")

        @pl.when(p == 6)
        def _():
            sides(turn, cold, warm, (1, 2), "wait_recv")

    flux_ref[...] = jnp.zeros_like(flux_ref)

    def second(p, carry):
        x = outer_third(p)
        takes_before(p, 0, cold_a, warm_a)
        flux = flux_ref[...]
        for r in row_groups(p):
            code = [bits[x, z, pl.ds(r, ROWS), :] for z in range(2)]
            rest = [cold_a[1, 1, 1, x + 1, z, pl.ds(r + ROWS, ROWS), :] for z in range(2)]
            sums, diffs = [], []
            for a, b, e in PAIRS:
                ahead = arrive(cold_a, x, r, code, (a, b, e))
                back = arrive(cold_a, x, r, code, (-a, -b, -e))
                sums.append([ahead[z] + back[z] for z in range(2)])
                diffs.append([ahead[z] - back[z] for z in range(2)])
            heat = [arrive_heat(warm_a, x, r, j) for j in range(7)]
            for z in range(2):
                fluid = kind[x + 1, z, pl.ds(r + ROWS, ROWS), :] == 0
                out_rest, pairs, hot = collide(
                    rest[z], [s[z] for s in sums], [d[z] for d in diffs], [g[z] for g in heat], fluid
                )
                store(cold_b, warm_b, x, r, z, out_rest, pairs, hot)
                terms = []
                for j in range(1, 7):
                    was = warm_a[j, x + 1, z, pl.ds(r + ROWS, ROWS), :]
                    terms.append(weights[j - 1, x, z, pl.ds(r, ROWS), :] * (was + hot[j]))
                flux = flux + tree(terms)
        flux_ref[...] = flux
        wall_rows(warm_b, x)

        @pl.when(p == 5)
        def _():
            faces(1, cold_b, warm_b, "start")

        @pl.when(p == planes // 2 - 1)
        def _():
            sides(1, cold_b, warm_b, (0, 3), "start")

        return carry

    lax.fori_loop(0, planes, second, 0)

    def sum_copy(slots, stage, at, target):
        return pltpu.make_async_remote_copy(
            src_ref=slots.at[at], dst_ref=slots.at[at],
            send_sem=sum_send.at[stage], recv_sem=sum_recv.at[stage],
            device_id=target, device_id_type=MESH,
        )

    def column_all():
        return sum_copy(meet_column, 0, pl.ds(0, columns - 1), column_device(1))

    def layer_all():
        return sum_copy(meet_layer, 1, pl.ds(0, layers - 1), layer_device(1))

    meet_column[column_index] = flux_ref[...]
    for d in range(1, columns):
        sum_copy(meet_column, 0, column_index, column_device(d)).start()
    sides(1, cold_b, warm_b, (1, 2), "start")

    def third(p, carry):
        x = outer_third(p)

        @pl.when(p == 6)
        def _():
            column_all().wait_recv()
            meet_layer[layer_index] = tree([meet_column[n] for n in range(columns)])
            for d in range(1, layers):
                sum_copy(meet_layer, 1, layer_index, layer_device(d)).start()

        takes_before(p, 1, cold_b, warm_b)
        for r in row_groups(p):
            code = [bits[x, z, pl.ds(r, ROWS), :] for z in range(2)]
            for a in (-1, 0, 1):
                for b in (-1, 0, 1):
                    for e in (-1, 0, 1):
                        i = 9 * (a + 1) + 3 * (b + 1) + (e + 1)
                        if i == 13:
                            value = [cold_b[1, 1, 1, x + 1, z, pl.ds(r + ROWS, ROWS), :] for z in range(2)]
                        else:
                            value = arrive(cold_b, x, r, code, (a, b, e))
                        for z in range(2):
                            flow_buf[i, x, pl.ds(r, ROWS), pl.ds(z * LANES, LANES)] = value[z]
            for j in range(7):
                value = arrive_heat(warm_b, x, r, j)
                for z in range(2):
                    heat_buf[j, x, pl.ds(r, ROWS), pl.ds(z * LANES, LANES)] = value[z]

        return carry

    lax.fori_loop(0, planes, third, 0)

    layer_all().wait_recv()
    flux_out[...] = tree([meet_layer[n] for n in range(layers)])

    column_all().wait_send()
    layer_all().wait_send()
    for n, dx, dy in kind_list:
        inside(dy, kind_copy(n, dx, dy).wait_send)
    for turn, cold, warm in ((0, cold_a, warm_a), (1, cold_b, warm_b)):
        faces(turn, cold, warm, "wait_send")
        sides(turn, cold, warm, (None,), "wait_send")


def out_kernel(cells, flow_ref, heat_ref, flux_ref, flow_out, heat_out, total_out, sem):
    copies = [
        pltpu.make_async_copy(flow_ref, flow_out, sem.at[0]),
        pltpu.make_async_copy(heat_ref, heat_out, sem.at[1]),
    ]
    for copy in copies:
        copy.start()
    total_out[0, 0] = jnp.sum(flux_ref[...]) * (1.0 / cells)
    for copy in copies:
        copy.wait()


def per_device(nx, ny, flow, heat, kind):
    _, planes, height, length = flow.shape
    assert length == 2 * LANES and height % ROWS == 0 and planes == 16
    assert nx % NEAR == 0 and ny % (2 * NEAR) == 0
    padded = (planes + 2, 2, height + 2 * ROWS, LANES)
    cold, warm = (3, 3, 3) + padded, (7,) + padded
    f32, i32 = jnp.float32, jnp.int32
    flow_new, heat_new, flux = pl.pallas_call(
        functools.partial(step_kernel, nx, ny),
        out_shape=(
            pltpu.VMEM(flow.shape, f32),
            pltpu.VMEM(heat.shape, f32),
            pltpu.VMEM((ROWS, LANES), f32),
        ),
        in_specs=[pl.BlockSpec(memory_space=pl.ANY)] * 3,
        out_specs=[pl.BlockSpec(memory_space=pltpu.VMEM)] * 3,
        scratch_shapes=[
            pltpu.VMEM(padded, i32),
            pltpu.VMEM((planes, 2, height, LANES), i32),
            pltpu.VMEM((6, planes, 2, height, LANES), f32),
            pltpu.VMEM(cold, f32),
            pltpu.VMEM(cold, f32),
            pltpu.VMEM(warm, f32),
            pltpu.VMEM(warm, f32),
            pltpu.VMEM((nx * ny // (NEAR * NEAR), ROWS, LANES), f32),
            pltpu.VMEM((NEAR * NEAR, ROWS, LANES), f32),
            pltpu.VMEM((ROWS, LANES), f32),
            pltpu.SemaphoreType.DMA((2, planes // 2)),
            pltpu.SemaphoreType.DMA((2,)),
            pltpu.SemaphoreType.DMA((2, 12)),
            pltpu.SemaphoreType.DMA((2, 24)),
            pltpu.SemaphoreType.DMA((8,)),
            pltpu.SemaphoreType.DMA((8,)),
            pltpu.SemaphoreType.DMA((2,)),
            pltpu.SemaphoreType.DMA((2,)),
        ],
        compiler_params=pltpu.CompilerParams(
            collective_id=0, has_side_effects=True, vmem_limit_bytes=44 * 1024 * 1024
        ),
    )(*[pltpu.with_memory_space_constraint(v, pltpu.HBM) for v in (flow, heat, kind)])
    cells = float(planes * nx * height * ny)
    flow_new, heat_new, total = pl.pallas_call(
        functools.partial(out_kernel, cells),
        out_shape=(
            jax.ShapeDtypeStruct(flow.shape, f32),
            jax.ShapeDtypeStruct(heat.shape, f32),
            jax.ShapeDtypeStruct((1, 1), f32),
        ),
        in_specs=[pl.BlockSpec(memory_space=pltpu.VMEM)] * 3,
        out_specs=[
            pl.BlockSpec(memory_space=pl.ANY),
            pl.BlockSpec(memory_space=pl.ANY),
            pl.BlockSpec(memory_space=pltpu.SMEM),
        ],
        scratch_shapes=[pltpu.SemaphoreType.DMA((2,))],
        compiler_params=pltpu.CompilerParams(vmem_limit_bytes=1024 * 1024),
    )(*[pltpu.with_memory_space_constraint(v, pltpu.VMEM) for v in (flow_new, heat_new, flux)])
    return flow_new, heat_new, total[0, 0]


def solution(mesh):
    return jax.shard_map(
        functools.partial(per_device, mesh.shape["gx"], mesh.shape["gy"]),
        mesh=mesh,
        in_specs=(P(None, "gx", "gy", None), P(None, "gx", "gy", None), P("gx", "gy", None)),
        out_specs=(P(None, "gx", "gy", None), P(None, "gx", "gy", None), P()),
        check_vma=False,
    )
```

time: 45.3 us -> 35.3 us (0.78)
  Pallas kernels: 44.6 us -> 34.5 us
    pallas_call x1, Pallas kernels: 40.5 us -> 30.4 us  [per_device(): pl.pallas_call(functools.partial(step_kernel, nx, ny), out_shape=(pltpu.V...]
where the time goes in v1:
time: 35.3 us; the launch traced here: 35.1 us
  Pallas kernels  34.5 us (98%)
  between operations  0.64 us (2%)
    pallas_call x1, Pallas kernels, per_device(): pl.pallas_call(functools.partial(step_kernel, nx, ny), out_shape=(pltpu.V...  30.4 us
    pallas_call x1, Pallas kernels, per_device(): pl.pallas_call(functools.partial(out_kernel, cells), out_shape=(jax.Shape...  4.09 us

profile of v1, /device:TPU:1, one launch (start us, length us, event | category | flops | bytes accessed | tf_op | source)
XLA Modules:
  0.0 35.1 jit_solution(7342010610436045833)
XLA Ops:
  0.6 30.4 %shard_map.58 = (f32[27,16,16,256]{3,2,1,0:T(8,128)S(1)}, f32[7,16,16,256]{3,2,1,0:T(8,128)S(1)}, f32[8,128]{1,0:T(8,128)S(1)}) custom-call(f32[27,16,16,256]{3,2,1,0:T(8,128)} %flow_hbm.1, f32[7,16,16,256]{3,2,1,0:T(8,128)} %heat_hbm.1, s32[16,16,256]{2,1,0:T(8,128)} %kind_hbm.1), custom_call_target="tpu_custom_call" | custom-call | tf_op jit(solution)/shard_map/pallas_call | solution.py:550
  31.0 4.1 %shard_map.59 = (f32[27,16,16,256]{3,2,1,0:T(8,128)}, f32[7,16,16,256]{3,2,1,0:T(8,128)}, f32[1,1]{1,0:T(1,128)}) custom-call(f32[27,16,16,256]{3,2,1,0:T(8,128)S(1)} %get-tuple-element.9.flow_ref, f32[7,16,16,256]{3,2,1,0:T(8,128)S(1)} %get-tuple-element.10.heat_ref, f32[8,128]{1,0:T(8,128)S(1)} %get-tuple-element.11.flux_ref), custom_call_target="tpu_custom_call" | custom-call | tf_op jit(solution)/shard_map/pallas_call | solution.py:584

commit v2 on v1

--- a/solution.py
+++ b/solution.py
@@ -158,6 +158,29 @@
         else:
             act()
 
+    along, across = gx // NEAR, lax.rem(gx, NEAR)
+    far, near, core = gy // (2 * NEAR), lax.rem(gy, 2 * NEAR) // 2, lax.rem(gy, 2)
+    fars = ny // (2 * NEAR)
+    columns = 2 * fars * (nx // NEAR)
+    layers = NEAR * NEAR
+    column_index = (along * fars + far) * 2 + core
+    layer_index = across * NEAR + near
+
+    def column_device(d):
+        n = lax.rem(column_index + d, columns)
+        return ((n // (2 * fars)) * NEAR + across, (lax.rem(n, 2 * fars) // 2) * 2 * NEAR + near * 2 + lax.rem(n, 2))
+
+    def layer_device(d):
+        n = lax.rem(layer_index + d, layers)
+        return (along * NEAR + n // NEAR, far * 2 * NEAR + lax.rem(n, NEAR) * 2 + core)
+
+    barrier = pltpu.get_barrier_semaphore()
+    greeted = [device(dx, dy) for dx, dy in FACES + SIDES + CORNERS]
+    greeted += [column_device(d) for d in range(1, columns)]
+    greeted += [layer_device(d) for d in range(1, layers)]
+    for target in greeted:
+        pl.semaphore_signal(barrier, inc=1, device_id=target, device_id_type=MESH)
+
     kind_copies = [
         pltpu.make_async_copy(
             kind_hbm.at[:, :, pl.ds(z * LANES, LANES)],
@@ -180,29 +203,6 @@
         for copy in load(k) + load(planes // 2 - 1 - k):
             copy.start()
 
-    along, across = gx // NEAR, lax.rem(gx, NEAR)
-    far, near, core = gy // (2 * NEAR), lax.rem(gy, 2 * NEAR) // 2, lax.rem(gy, 2)
-    fars = ny // (2 * NEAR)
-    columns = 2 * fars * (nx // NEAR)
-    layers = NEAR * NEAR
-    column_index = (along * fars + far) * 2 + core
-    layer_index = across * NEAR + near
-
-    def column_device(d):
-        n = lax.rem(column_index + d, columns)
-        return ((n // (2 * fars)) * NEAR + across, (lax.rem(n, 2 * fars) // 2) * 2 * NEAR + near * 2 + lax.rem(n, 2))
-
-    def layer_device(d):
-        n = lax.rem(layer_index + d, layers)
-        return (along * NEAR + n // NEAR, far * 2 * NEAR + lax.rem(n, NEAR) * 2 + core)
-
-    barrier = pltpu.get_barrier_semaphore()
-    greeted = [device(dx, dy) for dx, dy in FACES + SIDES + CORNERS]
-    greeted += [column_device(d) for d in range(1, columns)]
-    greeted += [layer_device(d) for d in range(1, layers)]
-    for target in greeted:
-        pl.semaphore_signal(barrier, inc=1, device_id=target, device_id_type=MESH)
-
     for copy in kind_copies:
         copy.wait()
 
@@ -290,15 +290,19 @@
             copies = [c for g in gs for c in side_copies(turn, cold, warm, n, g)]
             inside(sign * SIDES[n][1], each(copies, what))
 
-    def store(cold, warm, x, r, z, rest, pairs, hot):
-        def at(value, target, c):
-            target[c + (x + 1, z, pl.ds(r + ROWS, ROWS), slice(None))] = value
-        at(rest, cold, (1, 1, 1))
+    def own(x, r, z):
+        return (x + 1, z, pl.ds(r + ROWS, ROWS), slice(None))
+
+    def store_flow(cold, x, r, z, rest, pairs):
+        here = own(x, r, z)
+        cold[(1, 1, 1) + here] = rest
         for (a, b, e), (ahead, back) in zip(PAIRS, pairs):
-            at(ahead, cold, (1 + a, 1 + b, 1 + e))
-            at(back, cold, (1 - a, 1 - b, 1 - e))
+            cold[(1 + a, 1 + b, 1 + e) + here] = ahead
+            cold[(1 - a, 1 - b, 1 - e) + here] = back
+
+    def store_heat(warm, x, r, z, hot):
         for j in range(7):
-            at(hot[j], warm, (j,))
+            warm[(j,) + own(x, r, z)] = hot[j]
 
     def wall_rows(warm, x):
         @pl.when(gy == 0)
@@ -353,7 +357,7 @@
             for copy in load(x // 2):
                 copy.wait()
 
-        @pl.when(p == 1)
+        @pl.when(p == 3)
         def _():
             pl.semaphore_wait(barrier, len(greeted))
             for n, dx, dy in kind_list:
@@ -368,10 +372,11 @@
                 sums = [values[i] + values[26 - i] for i in range(14, 27)]
                 diffs = [values[i] - values[26 - i] for i in range(14, 27)]
                 rest, pairs, hot = collide(values[13], sums, diffs, heat, fluid)
-                store(cold_a, warm_a, x, r, z, rest, pairs, hot)
+                store_flow(cold_a, x, r, z, rest, pairs)
+                store_heat(warm_a, x, r, z, hot)
         wall_rows(warm_a, x)
 
-        @pl.when(p == 1)
+        @pl.when(p == 3)
         def _():
             faces(0, cold_a, warm_a, "start")
 
@@ -426,7 +431,7 @@
 
     flux_ref[...] = jnp.zeros_like(flux_ref)
 
-    def second(p, carry):
+    def second(whole, p, carry):
         x = outer_third(p)
         takes_before(p, 0, cold_a, warm_a)
         flux = flux_ref[...]
@@ -445,7 +450,10 @@
                 out_rest, pairs, hot = collide(
                     rest[z], [s[z] for s in sums], [d[z] for d in diffs], [g[z] for g in heat], fluid
                 )
-                store(cold_b, warm_b, x, r, z, out_rest, pairs, hot)
+                if not whole:
+                    out_rest, pairs = rest[z], [(s[z], d[z]) for s, d in zip(sums, diffs)]
+                store_flow(cold_b, x, r, z, out_rest, pairs)
+                store_heat(warm_b, x, r, z, hot)
                 terms = []
                 for j in range(1, 7):
                     was = warm_a[j, x + 1, z, pl.ds(r + ROWS, ROWS), :]
@@ -454,17 +462,30 @@
         flux_ref[...] = flux
         wall_rows(warm_b, x)
 
-        @pl.when(p == 5)
-        def _():
-            faces(1, cold_b, warm_b, "start")
-
-        @pl.when(p == planes // 2 - 1)
-        def _():
-            sides(1, cold_b, warm_b, (0, 3), "start")
+        if whole:
+            @pl.when(p == 5)
+            def _():
+                faces(1, cold_b, warm_b, "start")
 
         return carry
 
-    lax.fori_loop(0, planes, second, 0)
+    def finish(p, carry):
+        x = outer_third(p)
+        for r in row_groups(p):
+            for z in range(2):
+                here = own(x, r, z)
+                sums = [cold_b[(1 + a, 1 + b, 1 + e) + here] for a, b, e in PAIRS]
+                diffs = [cold_b[(1 - a, 1 - b, 1 - e) + here] for a, b, e in PAIRS]
+                heat = [warm_b[(j,) + here] for j in range(7)]
+                fluid = kind[x + 1, z, pl.ds(r + ROWS, ROWS), :] == 0
+                rest, pairs, _ = collide(cold_b[(1, 1, 1) + here], sums, diffs, heat, fluid)
+                store_flow(cold_b, x, r, z, rest, pairs)
+        return carry
+
+    late = planes // 2
+    lax.fori_loop(0, late, functools.partial(second, True), 0)
+    sides(1, cold_b, warm_b, (0, 3), "start")
+    lax.fori_loop(late, planes, functools.partial(second, False), 0)
 
     def sum_copy(slots, stage, at, target):
         return pltpu.make_async_remote_copy(
@@ -479,20 +500,21 @@
     def layer_all():
         return sum_copy(meet_layer, 1, pl.ds(0, layers - 1), layer_device(1))
 
-    meet_column[column_index] = flux_ref[...]
+    meet_column[pl.ds(column_index, 1), :] = jnp.sum(flux_ref[...], axis=0, keepdims=True)
     for d in range(1, columns):
-        sum_copy(meet_column, 0, column_index, column_device(d)).start()
+        sum_copy(meet_column, 0, pl.ds(column_index, 1), column_device(d)).start()
+    lax.fori_loop(late, planes, finish, 0)
     sides(1, cold_b, warm_b, (1, 2), "start")
 
     def third(p, carry):
         x = outer_third(p)
 
-        @pl.when(p == 6)
+        @pl.when(p == 0)
         def _():
             column_all().wait_recv()
-            meet_layer[layer_index] = tree([meet_column[n] for n in range(columns)])
+            meet_layer[pl.ds(layer_index, 1), :] = jnp.sum(meet_column[...], axis=0, keepdims=True)
             for d in range(1, layers):
-                sum_copy(meet_layer, 1, layer_index, layer_device(d)).start()
+                sum_copy(meet_layer, 1, pl.ds(layer_index, 1), layer_device(d)).start()
 
         takes_before(p, 1, cold_b, warm_b)
         for r in row_groups(p):
@@ -517,7 +539,7 @@
     lax.fori_loop(0, planes, third, 0)
 
     layer_all().wait_recv()
-    flux_out[...] = tree([meet_layer[n] for n in range(layers)])
+    flux_out[...] = tree([meet_layer[pl.ds(n * ROWS, ROWS), :] for n in range(layers // ROWS)])
 
     column_all().wait_send()
     layer_all().wait_send()
@@ -564,8 +586,8 @@
             pltpu.VMEM(cold, f32),
             pltpu.VMEM(warm, f32),
             pltpu.VMEM(warm, f32),
-            pltpu.VMEM((nx * ny // (NEAR * NEAR), ROWS, LANES), f32),
-            pltpu.VMEM((NEAR * NEAR, ROWS, LANES), f32),
+            pltpu.VMEM((nx * ny // (NEAR * NEAR), LANES), f32),
+            pltpu.VMEM((NEAR * NEAR, LANES), f32),
             pltpu.VMEM((ROWS, LANES), f32),
             pltpu.SemaphoreType.DMA((2, planes // 2)),
             pltpu.SemaphoreType.DMA((2,)),

time: 35.3 us -> 33.1 us (0.938)
  Pallas kernels: 34.5 us -> 32.2 us
    pallas_call x1, Pallas kernels: 30.4 us -> 28.1 us  [per_device(): pl.pallas_call(functools.partial(step_kernel, nx, ny), out_shape=(pltpu.V...]
where the time goes in v2:
time: 33.1 us; the launch traced here: 32.9 us
  Pallas kernels  32.2 us (97%)
  between operations  0.64 us (2%)
    pallas_call x1, Pallas kernels, per_device(): pl.pallas_call(functools.partial(step_kernel, nx, ny), out_shape=(pltpu.V...  28.1 us
    pallas_call x1, Pallas kernels, per_device(): pl.pallas_call(functools.partial(out_kernel, cells), out_shape=(jax.Shape...  4.09 us

profile of v2, /device:TPU:1, one launch (start us, length us, event | category | flops | bytes accessed | tf_op | source)
XLA Modules:
  0.0 32.9 jit_solution(3713567764190661354)
XLA Ops:
  0.6 28.1 %shard_map.58 = (f32[27,16,16,256]{3,2,1,0:T(8,128)S(1)}, f32[7,16,16,256]{3,2,1,0:T(8,128)S(1)}, f32[8,128]{1,0:T(8,128)S(1)}) custom-call(f32[27,16,16,256]{3,2,1,0:T(8,128)} %flow_hbm.1, f32[7,16,16,256]{3,2,1,0:T(8,128)} %heat_hbm.1, s32[16,16,256]{2,1,0:T(8,128)} %kind_hbm.1), custom_call_target="tpu_custom_call" | custom-call | tf_op jit(solution)/shard_map/pallas_call | solution.py:572
  28.8 4.1 %shard_map.59 = (f32[27,16,16,256]{3,2,1,0:T(8,128)}, f32[7,16,16,256]{3,2,1,0:T(8,128)}, f32[1,1]{1,0:T(1,128)}) custom-call(f32[27,16,16,256]{3,2,1,0:T(8,128)S(1)} %get-tuple-element.9.flow_ref, f32[7,16,16,256]{3,2,1,0:T(8,128)S(1)} %get-tuple-element.10.heat_ref, f32[8,128]{1,0:T(8,128)S(1)} %get-tuple-element.11.flux_ref), custom_call_target="tpu_custom_call" | custom-call | tf_op jit(solution)/shard_map/pallas_call | solution.py:606

commit v3 on v2

--- a/solution.py
+++ b/solution.py
@@ -538,16 +538,17 @@
 
     lax.fori_loop(0, planes, third, 0)
 
-    layer_all().wait_recv()
-    flux_out[...] = tree([meet_layer[pl.ds(n * ROWS, ROWS), :] for n in range(layers // ROWS)])
-
     column_all().wait_send()
-    layer_all().wait_send()
     for n, dx, dy in kind_list:
         inside(dy, kind_copy(n, dx, dy).wait_send)
     for turn, cold, warm in ((0, cold_a, warm_a), (1, cold_b, warm_b)):
         faces(turn, cold, warm, "wait_send")
         sides(turn, cold, warm, (None,), "wait_send")
+
+    layer_all().wait_recv()
+    flux_out[...] = tree([meet_layer[pl.ds(n * ROWS, ROWS), :] for n in range(layers // ROWS)])
+
+    layer_all().wait_send()
 
 
 def out_kernel(cells, flow_ref, heat_ref, flux_ref, flow_out, heat_out, total_out, sem):

time: 33.1 us -> 33.1 us (level)
  no operation moved by 1% of the time
where the time goes in v3:
time: 33.1 us; the launch traced here: 32.8 us
  Pallas kernels  32.2 us (97%)
  between operations  0.64 us (2%)
    pallas_call x1, Pallas kernels, per_device(): pl.pallas_call(functools.partial(step_kernel, nx, ny), out_shape=(pltpu.V...  28.1 us
    pallas_call x1, Pallas kernels, per_device(): pl.pallas_call(functools.partial(out_kernel, cells), out_shape=(jax.Shape...  4.09 us

profile of v3, /device:TPU:1, one launch (start us, length us, event | category | flops | bytes accessed | tf_op | source)
XLA Modules:
  0.0 32.8 jit_solution(1928711774977930327)
XLA Ops:
  0.6 28.1 %shard_map.58 = (f32[27,16,16,256]{3,2,1,0:T(8,128)S(1)}, f32[7,16,16,256]{3,2,1,0:T(8,128)S(1)}, f32[8,128]{1,0:T(8,128)S(1)}) custom-call(f32[27,16,16,256]{3,2,1,0:T(8,128)} %flow_hbm.1, f32[7,16,16,256]{3,2,1,0:T(8,128)} %heat_hbm.1, s32[16,16,256]{2,1,0:T(8,128)} %kind_hbm.1), custom_call_target="tpu_custom_call" | custom-call | tf_op jit(solution)/shard_map/pallas_call | solution.py:573
  28.7 4.1 %shard_map.59 = (f32[27,16,16,256]{3,2,1,0:T(8,128)}, f32[7,16,16,256]{3,2,1,0:T(8,128)}, f32[1,1]{1,0:T(1,128)}) custom-call(f32[27,16,16,256]{3,2,1,0:T(8,128)S(1)} %get-tuple-element.9.flow_ref, f32[7,16,16,256]{3,2,1,0:T(8,128)S(1)} %get-tuple-element.10.heat_ref, f32[8,128]{1,0:T(8,128)S(1)} %get-tuple-element.11.flux_ref), custom_call_target="tpu_custom_call" | custom-call | tf_op jit(solution)/shard_map/pallas_call | solution.py:607
